TPU v7x, 32 devices: a whole 2x2x4 slice. The times are simulated.
32 devices in a mesh: group: 2 (over y), fsdp: 4 (over z), seq: 2 (over x), proj: 2 (over core).
Axes of the slice: x: 2, y: 2, z: 4, core: 2. Of those that a mesh axis runs over, the one named last changes fastest.
Arguments:
- patches: bfloat16 [6144, 1280], P(('group', 'fsdp', 'seq')), parts along dimension 0, may hold values from -6 to 6
- cotangent: bfloat16 [6144, 1280], P(('group', 'fsdp', 'seq')), parts along dimension 0, may hold values from -6 to 6
- segment: int32 [6144], P(('group', 'fsdp', 'seq')), parts along dimension 0, may hold values from 0 to 7, never falling along the last dimension, each value on 1 to 768 neighbouring positions
- home_map: int32 [16], P('group'), parts along dimension 0, may hold values from 0 to 7, as said below
- ln_gain: float32 [1280], replicated, may hold values from 0.1 to 1.9
- w_up: bfloat16 [1280, 5120], P('fsdp', 'proj'), may hold values from -0.15625 to 0.15625
- w_down_t: bfloat16 [1280, 5120], P('fsdp', 'proj'), may hold values from -0.078125 to 0.078125
- p_in1: bfloat16 [1280, 32], replicated, may hold values from -0.15625 to 0.15625
- q_out1: bfloat16 [5120, 32], P('proj'), may hold values from -0.078125 to 0.078125
- p_in2: bfloat16 [5120, 32], P('proj'), may hold values from -0.078125 to 0.078125
- q_out2: bfloat16 [1280, 32], replicated, may hold values from -0.15625 to 0.15625
Outputs:
- gradients: float32 [16, 32, 64], P(('group', 'fsdp', 'seq'), 'proj'), parts along dimension 0
There are 2 independent parts, one for each index of `group`. A program takes and returns all parts, laid end to end along the dimension named above; an argument that names none is the same for every part. Nothing has to cross between parts.
Inputs may be any that keep to these rules, and one draw needn't show every extreme that they name: segment never falls along the patches and starts at 0; every image has 1 to 768 patches and one has exactly 768. home_map is a permutation of the rows; image 0 is homed at row 4.
All inputs are finite; a program needn't handle non-finite values.
Results may differ from a plain program's by a relative error of at most 0.0055.
Values may be sent and summed in bfloat16 or wider, within the bound.
A program may use at most 64 MiB of HBM per device.

v0:
```python
import jax
import jax.numpy as jnp
from jax import lax
from jax.sharding import PartitionSpec as P

EX_DEV = 1


def add_rows(left, piece):
    return jnp.dot(left, piece, preferred_element_type=jnp.float32)


def body(
    patches, cotangent, segment, home_map, ln_gain, w_up, w_down_t, p_in1, q_out1, p_in2, q_out2
):
    values = patches.astype(jnp.float32)
    center = values - jnp.mean(values, axis=-1, keepdims=True)
    spread = jnp.mean(center * center, axis=-1, keepdims=True)
    normed = (center * lax.rsqrt(spread + 1e-06) * ln_gain).astype(jnp.bfloat16)
    pre = add_rows(normed, lax.all_gather(w_up, "fsdp", axis=0, tiled=True))
    dact = add_rows(cotangent, lax.all_gather(w_down_t, "fsdp", axis=0, tiled=True))
    sigma = jax.nn.sigmoid(1.702 * pre)
    act = (pre * sigma).astype(jnp.bfloat16)
    dpre = (dact * (sigma + 1.702 * pre * sigma * (1.0 - sigma))).astype(jnp.bfloat16)
    in_one = jnp.dot(normed, p_in1, preferred_element_type=jnp.float32)
    out_one = jnp.dot(dpre, q_out1, preferred_element_type=jnp.float32)
    in_two = jnp.dot(act, p_in2, preferred_element_type=jnp.float32)
    out_two = jnp.dot(cotangent, q_out2, preferred_element_type=jnp.float32)
    images = EX_DEV * lax.axis_size("fsdp") * lax.axis_size("seq")
    proj_out = q_out1.shape[1]
    proj_in = p_in1.shape[1]
    rows = patches.shape[0]
    outer = jnp.concatenate(
        [out_one[:, :, None] * in_one[:, None, :], out_two[:, :, None] * in_two[:, None, :]], axis=2
    )
    outer = outer.reshape(rows, proj_out * 2 * proj_in)
    high_part = outer.astype(jnp.bfloat16)
    low_part = (outer - high_part.astype(jnp.float32)).astype(jnp.bfloat16)
    image_ids = jnp.arange(images, dtype=jnp.int32)
    owner = segment[:, None] == image_ids[None, :]
    target = jnp.sum(jnp.where(owner, home_map[None, :], 0), axis=1)
    member = target[:, None] == image_ids[None, :]
    onehot = member.astype(jnp.bfloat16)
    counts = jnp.sum(member.astype(jnp.float32), axis=0)
    dims = (((0,), (0,)), ((), ()))
    flat = lax.dot_general(onehot, high_part, dims, preferred_element_type=jnp.float32)
    flat = flat + lax.dot_general(onehot, low_part, dims, preferred_element_type=jnp.float32)
    split_rows = flat.reshape(images * 2, proj_out // 2, 2 * proj_in)
    paired = jnp.repeat(counts, 2)
    mine, totals = (
        lax.psum_scatter(split_rows, ("fsdp", "seq", "proj"), scatter_dimension=0, tiled=True),
        lax.psum_scatter(paired, ("fsdp", "seq", "proj"), scatter_dimension=0, tiled=True),
    )
    result = mine[0] * lax.rsqrt(totals * 0.5)[0]
    return result.reshape(1, result.shape[0], result.shape[1])


def solution(mesh):
    return jax.shard_map(
        body,
        mesh=mesh,
        in_specs=(
            P(("group", "fsdp", "seq"), None),
            P(("group", "fsdp", "seq"), None),
            P(("group", "fsdp", "seq")),
            P("group"),
            P(),
            P("fsdp", "proj"),
            P("fsdp", "proj"),
            P(),
            P("proj", None),
            P("proj", None),
            P(),
        ),
        out_specs=P(("group", "fsdp", "seq"), "proj", None),
        check_vma=False,
    )
```

profile of v0, /device:TPU:0, one launch (start us, length us, event | category | flops | bytes accessed | tf_op | source)
XLA Modules:
  0.0 322.2 jit_solution(12455325566822334351)
XLA Ops:
  6.5 0.0 all-gather.5.cloned.1.call-start
  6.6 0.7 all-gather.5.cloned.1.call-update
  7.3 0.0 all-gather.3.cloned.1.call-start
  7.3 0.7 all-gather.3.cloned.1.call-update
  8.1 0.0 reduce-scatter.2.cloned.1.call-start
  8.1 0.1 select_reduce_fusion
  8.2 0.2 convert_reduce_fusion
  8.4 0.4 fusion.4
  8.9 0.4 fusion.20
  9.2 0.0 copy-done.7
  9.3 0.5 fusion.16
  9.8 121.5 %all-gather.5.cloned.1.call-done = bf16[1280,2560]{1,0:T(8,128)(2,1)} async-done(((bf16[320,2560]{1,0:T(8,128)(2,1)}), bf16[1280,2560]{1,0:T(8,128)(2,1)}) %all-gather.5.cloned.1.call-update) | async-done | bytes 6553616 | tf_op jit(solution)/shard_map/all_gather | solution.py:20
  131.3 5.0 %fusion.18 = f32[384,2560]{1,0:T(8,128)S(1)} fusion(bf16[1280,2560]{1,0:T(8,128)(2,1)} %all-gather.5.cloned.1.call-done, bf16[384,1280]{1,0:T(8,128)(2,1)S(1)} %copy-done.1, f32[1280]{0:T(1024)S(1)} %copy-done.8, f32[384]{0:T(512)S(1)} %add_rsqrt_fusion, f32[384]{0:T(512)S(1)} %broadcast_multiply_fusion.3), kind=kOutput, calls=%fused_computation.35 | convolution fusion | flops 2519040000 | bytes 11476992 | tf_op jit(solution)/shard_map/dot_general | solution.py:10
  136.3 1.9 copy-done.10
  138.3 1.1 fusion.7
  139.4 111.4 %all-gather.3.cloned.1.call-done = bf16[1280,2560]{1,0:T(8,128)(2,1)} async-done(((bf16[320,2560]{1,0:T(8,128)(2,1)}), bf16[1280,2560]{1,0:T(8,128)(2,1)}) %all-gather.3.cloned.1.call-update) | async-done | bytes 6553616 | tf_op jit(solution)/shard_map/all_gather | solution.py:21
  250.8 7.2 %fusion.8 = f32[384,32]{0,1:T(8,128)S(1)} fusion(bf16[2560,32]{0,1:T(8,128)(2,1)S(1)} %copy-done.6, bf16[384,1280]{1,0:T(8,128)(2,1)S(1)} %copy-done, bf16[1280,2560]{1,0:T(8,128)(2,1)} %all-gather.3.cloned.1.call-done, f32[384,2560]{1,0:T(8,128)} %copy-done.10), kind=kOutput, calls=%fused_computation.17 | convolution fusion | flops 2589327360 | bytes 11681792 | tf_op jit(solution)/shard_map/dot_general | solution.py:26
  258.0 0.2 broadcast_multiply_fusion.1
  258.2 0.2 broadcast_multiply_fusion
  258.4 0.3 pad_maximum_fusion
  258.7 0.4 fusion.1
  259.1 0.5 fusion.9
  259.6 0.5 convolution_add_fusion
  260.2 0.7 reshape.31
  260.9 0.1 convert_reduce_fusion.1
  261.0 0.1 broadcast_in_dim.12
  261.1 0.1 reshape.32
  261.2 30.6 %all-reduce = f32[16]{0:T(128)S(1)} all-reduce(f32[16]{0:T(128)S(1)} %reshape.32), channel_id=3, replica_groups=mesh['group'=2,'fsdp'=4,'seq'=2,'proj'=2] {'fsdp','seq','proj'}, use_global_device_ids=true, to_apply=%region_5.6.clone | all-reduce | flops 16 | bytes 128
  291.8 0.6 dynamic-slice
  292.3 1.3 dynamic-slice.1
  294.3 20.1 %reduce-scatter.2.cloned.1.call-done = f32[1,16,64]{2,1,0:T(8,128)} async-done(((f32[16,16,64]{2,1,0:T(8,128)}), f32[1,16,64]{2,1,0:T(8,128)}) %reduce-scatter.2.cloned.1.call-update) | async-done | bytes 4112 | tf_op jit(solution)/shard_map/reduce_scatter | solution.py:51
  314.4 1.3 broadcast_multiply_fusion.2
  (23 shorter events, 0.1 us)
Async XLA Ops:
  6.5 2.3 copy-start
  6.5 1.6 copy-start.3
  6.5 1.6 copy-start.4
  6.5 1.7 copy-start.1
  6.5 124.8 %all-gather.5.cloned.1.call-start = ((), (), s32[]{:S(2)}) async-start(), calls=%async_computation.2 | async-start | bytes 8192000 | tf_op jit(solution)/shard_map/all_gather | solution.py:20
  7.3 1.6 copy-start.2
  7.3 2.0 copy-start.7
  7.3 2.0 copy-start.8
  7.3 243.5 %all-gather.3.cloned.1.call-start = ((), (), s32[]{:S(2)}) async-start(), calls=%async_computation.1 | async-start | bytes 8192000 | tf_op jit(solution)/shard_map/all_gather | solution.py:21
  8.1 306.3 %reduce-scatter.2.cloned.1.call-start = ((), (), s32[]{:S(2)}) async-start(), calls=%async_computation.3 | async-start | bytes 139264 | tf_op jit(solution)/shard_map/reduce_scatter | solution.py:51
  9.8 128.5 %copy-start.5 = (bf16[2560,32]{0,1:T(8,128)(2,1)S(1)}, bf16[2560,32]{0,1:T(8,128)(2,1)}, u32[]{:S(2)}) copy-start(bf16[2560,32]{0,1:T(8,128)(2,1)} %param.20) | copy-start | bytes 491524
  136.3 1.9 copy-start.10
  138.3 112.5 %copy-start.6 = (bf16[2560,32]{0,1:T(8,128)(2,1)S(1)}, bf16[2560,32]{0,1:T(8,128)(2,1)}, u32[]{:S(2)}) copy-start(bf16[2560,32]{0,1:T(8,128)(2,1)} %param.19) | copy-start | bytes 491524
  259.1 32.7 %copy-start.9 = (u32[32]{0:T(128)S(1)}, u32[32]{0:T(128)}, u32[]{:S(2)}) copy-start(u32[32]{0:T(128)} %constant.18) | copy-start | bytes 388
Sparse Core Ops, SparseCore 0:
  8.9 122.3 all-gather.4
  132.9 117.8 all-gather.2
  261.0 53.2 reduce-scatter.1
where the time goes:
time: 322 us
  waiting for transfers between devices  254 us (79%)
  blocking collectives  30.6 us (10%)
  matrix products  15.3 us (5%)
  between operations  14 us (4%)
  local copies, waits for them, and re-layouts  4.71 us (1%)
    all_gather x1, waiting for transfers between devices, body(): pre = add_rows(normed, lax.all_gather(w_up, 'fsdp', axis=0, tiled=True))  122 us
    all_gather x1, waiting for transfers between devices, body(): lax.all_gather(w_down_t, 'fsdp', axis=0, tiled=True)  111 us
    unnamed x1, blocking collectives  30.6 us
    reduce_scatter x1, waiting for transfers between devices, body(): lax.psum_scatter(split_rows, ('fsdp', 'seq', 'proj'), scatter_dimension=0...  20.1 us
    dot_general x1, matrix products, body(): out_one = jnp.dot(dpre, q_out1, preferred_element_type=jnp.float32)  7.23 us
  transfers between devices with their start and end apart: 3, of which 3 were waited for; matrix products, arithmetic and copies ran while one was open for 3% of the time, Pallas kernels for 0%

commit v1 on v0

v1 whole, which is shorter than its diff:
```python
import functools

import jax
import jax.numpy as jnp
from jax import lax
from jax.experimental import pallas as pl
from jax.experimental.pallas import tpu as pltpu
from jax.sharding import PartitionSpec as P

KC = 256
HC = 128
MESH = pl.DeviceIdType.MESH
BF = jnp.bfloat16
F32 = jnp.float32
NT = (((1,), (1,)), ((), ()))


def kernel(
    fn, sn, chunks,
    patches, cot, seg, home, gain, w_up, w_down, p_in1, q_out1, p_in2, q_out2,
    out,
    pbuf, xbuf, sbuf, wbuf, p1v, q1v, p2v, q2v,
    p1p, p2p, q1t, q2t, in1, in2, t1, t2, part, gath,
    lsem, wsem, zrecv, yrecv, rsend, lsend, ysend, xsem, seg_sem, csem, red_send, red_recv,
):
    g, f = lax.axis_index("group"), lax.axis_index("fsdp")
    s, p = lax.axis_index("seq"), lax.axis_index("proj")
    s2 = lax.rem(s, 2)
    mate = s + 1 - 2 * s2
    n = fn * sn * 2
    me = (f * sn + s) * 2 + p
    rows, width = patches.shape
    half = rows // 2
    depth = w_up.shape[0]
    images = home.shape[0]
    ko = q_out1.shape[1]
    ki = p_in1.shape[1]
    cols = chunks * KC
    base = pl.multiple_of(s2 * cols, KC)

    def spot(linear):
        return {"fsdp": linear // (2 * sn), "seq": lax.rem(linear // 2, sn), "proj": lax.rem(linear, 2)}

    own_rows = pl.ds(0, rows)
    loads = [
        pltpu.make_async_copy(patches, pbuf, lsem.at[0]),
        pltpu.make_async_copy(cot, xbuf.at[1, own_rows], lsem.at[1]),
        pltpu.make_async_copy(q_out1.at[pl.ds(base, cols)], q1v, lsem.at[2]),
        pltpu.make_async_copy(p_in2.at[pl.ds(base, cols)], p2v, lsem.at[3]),
        pltpu.make_async_copy(p_in1, p1v, lsem.at[4]),
        pltpu.make_async_copy(q_out2, q2v, lsem.at[5]),
    ]

    def own_load(k, m):
        source = (w_up, w_down)[m]
        columns = pl.ds(pl.multiple_of(base + k * KC, KC), KC)
        return pltpu.make_async_copy(
            source.at[:, columns], wbuf.at[k, m, pl.ds(pl.multiple_of(f * depth, depth), depth)], wsem.at[k, m]
        )

    for k in range(chunks):
        for m in range(2):
            own_load(k, m).start()
        if k == 0:
            loads[0].start()
            loads[1].start()
    for load in loads[2:]:
        load.start()
    sbuf[0] = jnp.broadcast_to(seg[...], sbuf.shape[1:])

    barrier = pltpu.get_barrier_semaphore()

    def greet(o, carry):
        pl.semaphore_signal(barrier, inc=1, device_id=spot(lax.rem(me + o, n)), device_id_type=MESH)
        return carry

    lax.fori_loop(1, n, greet, 0)
    pl.semaphore_signal(barrier, inc=1, device_id={"group": 1 - g}, device_id_type=MESH)
    pl.semaphore_wait(barrier, n)

    def piece(k, source, side):
        return wbuf.at[
            k, :, pl.ds(pl.multiple_of(source * depth, depth), depth), pl.ds(pl.multiple_of(side * HC, HC), HC)
        ]

    def z_copy(k, source, way):
        sems = rsend if way > 0 else lsend
        block = piece(k, source, g)
        return pltpu.make_async_remote_copy(
            src_ref=block, dst_ref=block, send_sem=sems.at[k, source], recv_sem=zrecv.at[k, source],
            device_id={"fsdp": f + way}, device_id_type=MESH,
        )

    def y_copy(k, source, side):
        block = piece(k, source, side)
        return pltpu.make_async_remote_copy(
            src_ref=block, dst_ref=block, send_sem=ysend.at[k, source], recv_sem=yrecv.at[k, source],
            device_id={"group": 1 - g}, device_id_type=MESH,
        )

    def send_own(k):
        for m in range(2):
            own_load(k, m).wait()

        @pl.when(f < fn - 1)
        def _():
            z_copy(k, f, 1).start()

        @pl.when(f > 0)
        def _():
            z_copy(k, f, -1).start()

    def forward(k):
        for d in range(1, fn):
            @pl.when(f - d >= 0)
            def _():
                z_copy(k, f - d, 1).wait_recv()

                @pl.when(f < fn - 1)
                def _():
                    z_copy(k, f - d, 1).start()

                y_copy(k, f - d, g).start()

            @pl.when(f + d < fn)
            def _():
                z_copy(k, f + d, -1).wait_recv()

                @pl.when(f > 0)
                def _():
                    z_copy(k, f + d, -1).start()

                y_copy(k, f + d, g).start()

    send_own(0)
    send_own(1)

    def x_copy():
        mine = pl.ds(pl.multiple_of(p * half, half), half)
        there = pl.ds(pl.multiple_of(rows + p * half, half), half)
        return pltpu.make_async_remote_copy(
            src_ref=xbuf.at[:, mine], dst_ref=xbuf.at[:, there], send_sem=xsem.at[0], recv_sem=xsem.at[1],
            device_id={"seq": mate}, device_id_type=MESH,
        )

    def c_copy(side):
        block = xbuf.at[:, pl.ds(pl.multiple_of(rows + side * half, half), half)]
        return pltpu.make_async_remote_copy(
            src_ref=block, dst_ref=block, send_sem=csem.at[0], recv_sem=csem.at[1],
            device_id={"proj": 1 - p}, device_id_type=MESH,
        )

    seg_copy = pltpu.make_async_remote_copy(
        src_ref=sbuf.at[0], dst_ref=sbuf.at[1], send_sem=seg_sem.at[0], recv_sem=seg_sem.at[1],
        device_id={"seq": mate}, device_id_type=MESH,
    )
    seg_copy.start()

    loads[0].wait()
    step = 32

    def norm(i, carry):
        at = pl.ds(pl.multiple_of(i * step, step), step)
        values = pbuf[at, :].astype(F32)
        center = values - jnp.mean(values, axis=-1, keepdims=True)
        spread = jnp.mean(center * center, axis=-1, keepdims=True)
        xbuf[0, at, :] = (center * lax.rsqrt(spread + 1e-06) * gain[...]).astype(BF)
        return carry

    lax.fori_loop(0, rows // step, norm, 0)
    loads[1].wait()
    x_copy().start()

    for load in loads[2:]:
        load.wait()

    def pick(shape, shift):
        i = lax.broadcasted_iota(jnp.int32, shape, 0)
        j = lax.broadcasted_iota(jnp.int32, shape, 1)
        return (j == i + shift).astype(BF)

    p1p[...] = jnp.dot(p1v[...], pick((ki, 128), 0), preferred_element_type=F32).astype(BF)
    p2p[...] = jnp.dot(p2v[...], pick((ki, 128), ki), preferred_element_type=F32).astype(BF)
    eye = pick((ko, ko), 0)
    q2t[...] = lax.dot_general(eye, q2v[...], NT, preferred_element_type=F32).astype(BF)
    for k in range(chunks):
        q1t[k] = lax.dot_general(
            eye, q1v[k * KC:(k + 1) * KC, :], NT, preferred_element_type=F32
        ).astype(BF)

    def small(r):
        at = pl.ds(r * rows, rows)
        in1[r] = jnp.dot(xbuf[0, at, :], p1p[...], preferred_element_type=F32)
        t2[r] = lax.dot_general(q2t[...], xbuf[1, at, :], NT, preferred_element_type=F32)

    def compute(k):
        for d in range(1, fn):
            @pl.when(f - d >= 0)
            def _():
                y_copy(k, f - d, 1 - g).wait_recv()

            @pl.when(f + d < fn)
            def _():
                y_copy(k, f + d, 1 - g).wait_recv()

        def rows_of(r, carry):
            at = pl.ds(pl.multiple_of(r * rows, rows), rows)
            pre = jnp.dot(xbuf[0, at, :], wbuf[k, 0], preferred_element_type=F32)
            dact = jnp.dot(xbuf[1, at, :], wbuf[k, 1], preferred_element_type=F32)
            sigma = 0.5 + 0.5 * jnp.tanh(0.851 * pre)
            act = (pre * sigma).astype(BF)
            dpre = (dact * (sigma * (1.0 + 1.702 * pre * (1.0 - sigma)))).astype(BF)
            two = jnp.dot(act, p2p[k * KC:(k + 1) * KC, :], preferred_element_type=F32)
            one = lax.dot_general(q1t[k], dpre, NT, preferred_element_type=F32)
            if k == 0:
                in2[r] = two
                t1[r] = one
            else:
                in2[r] += two
                t1[r] += one
            return carry

        lax.fori_loop(0, 2, rows_of, 0)

    small(0)
    forward(0)
    send_own(2)
    forward(1)
    send_own(3)
    x_copy().wait_recv()
    c_copy(p).start()
    seg_copy.wait_recv()
    c_copy(1 - p).wait_recv()
    small(1)
    compute(0)
    forward(2)
    send_own(4)
    compute(1)
    forward(3)
    compute(2)
    forward(4)
    compute(3)
    compute(4)

    goal = []
    for r in range(2):
        ids = sbuf[r, 0:1, :]
        goal.append(lax.fori_loop(
            0, images, lambda e, t: jnp.where(ids == e, home[e], t), jnp.zeros_like(ids)
        ))
    lane = lax.broadcasted_iota(jnp.int32, (ko // 2, 128), 1)
    many = 8

    def blocks(b, carry):
        raw = jnp.zeros((many * ko, 128), F32)
        counts = [jnp.zeros((1, 1), F32) for _ in range(many)]
        for r in range(2):
            marks = [(goal[r] == b * many + j).astype(F32) for j in range(many)]
            counts = [c + jnp.sum(m, axis=1, keepdims=True) for c, m in zip(counts, marks)]
            left1 = jnp.concatenate([t1[r] * m for m in marks], axis=0)
            left2 = jnp.concatenate([t2[r] * m for m in marks], axis=0)
            raw += jnp.dot(left1, in1[r], preferred_element_type=F32, precision=lax.Precision.HIGHEST)
            raw += jnp.dot(left2, in2[r], preferred_element_type=F32, precision=lax.Precision.HIGHEST)
        for j in range(many):
            for c in range(2):
                start = j * ko + c * (ko // 2)
                part[(b * many + j) * 2 + c] = jnp.where(
                    lane == 2 * ki, counts[j], raw[start:start + ko // 2]
                )
        return carry

    lax.fori_loop(0, images // many, blocks, 0)

    def give(o):
        target = lax.rem(me + o, n)
        return pltpu.make_async_remote_copy(
            src_ref=part.at[target], dst_ref=gath.at[me], send_sem=red_send.at[target], recv_sem=red_recv.at[me],
            device_id=spot(target), device_id_type=MESH,
        )

    def take(o):
        origin = lax.rem(me + n - o, n)
        return origin, pltpu.make_async_remote_copy(
            src_ref=part.at[origin], dst_ref=gath.at[origin], send_sem=red_send.at[origin],
            recv_sem=red_recv.at[origin], device_id=spot(origin), device_id_type=MESH,
        )

    def start(o, carry):
        give(o).start()
        return carry

    lax.fori_loop(1, n, start, 0)

    def finish(o, total):
        origin, copy = take(o)
        copy.wait_recv()
        return total + gath[origin]

    total = lax.fori_loop(1, n, finish, part[me])
    out[0] = total[:, :2 * ki] * lax.rsqrt(total[:, 2 * ki:2 * ki + 1] * 0.25)

    def drain(o, carry):
        give(o).wait_send()
        return carry

    lax.fori_loop(1, n, drain, 0)
    x_copy().wait_send()
    c_copy(p).wait_send()
    seg_copy.wait_send()
    for k in range(chunks):
        @pl.when(f < fn - 1)
        def _():
            z_copy(k, f, 1).wait_send()

        @pl.when(f > 0)
        def _():
            z_copy(k, f, -1).wait_send()

        for d in range(1, fn):
            @pl.when(f - d >= 0)
            def _():
                @pl.when(f < fn - 1)
                def _():
                    z_copy(k, f - d, 1).wait_send()

                y_copy(k, f - d, g).wait_send()

            @pl.when(f + d < fn)
            def _():
                @pl.when(f > 0)
                def _():
                    z_copy(k, f + d, -1).wait_send()

                y_copy(k, f + d, g).wait_send()


def body(
    patches, cotangent, segment, home_map, ln_gain, w_up, w_down_t, p_in1, q_out1, p_in2, q_out2
):
    fn, sn = lax.axis_size("fsdp"), lax.axis_size("seq")
    n = fn * sn * 2
    rows, width = patches.shape
    cols = w_up.shape[1] // 2
    chunks = cols // KC
    ko, ki = q_out1.shape[1], p_in1.shape[1]
    any_ = pl.BlockSpec(memory_space=pl.ANY)
    vmem = pl.BlockSpec(memory_space=pltpu.VMEM)
    smem = pl.BlockSpec(memory_space=pltpu.SMEM)
    dma = pltpu.SemaphoreType.DMA
    return pl.pallas_call(
        functools.partial(kernel, fn, sn, chunks),
        out_shape=jax.ShapeDtypeStruct((1, ko // 2, 2 * ki), F32),
        in_specs=[any_, any_, vmem, smem, vmem, any_, any_, any_, any_, any_, any_],
        out_specs=vmem,
        scratch_shapes=[
            pltpu.VMEM((rows, width), BF),
            pltpu.VMEM((2, 2 * rows, width), BF),
            pltpu.VMEM((2, 8, rows), jnp.int32),
            pltpu.VMEM((chunks, 2, width, KC), BF),
            pltpu.VMEM((width, ki), BF),
            pltpu.VMEM((cols, ko), BF),
            pltpu.VMEM((cols, ki), BF),
            pltpu.VMEM((width, ko), BF),
            pltpu.VMEM((width, 128), BF),
            pltpu.VMEM((cols, 128), BF),
            pltpu.VMEM((chunks, ko, KC), BF),
            pltpu.VMEM((ko, width), BF),
            pltpu.VMEM((2, rows, 128), F32),
            pltpu.VMEM((2, rows, 128), F32),
            pltpu.VMEM((2, ko, rows), F32),
            pltpu.VMEM((2, ko, rows), F32),
            pltpu.VMEM((n, ko // 2, 128), F32),
            pltpu.VMEM((n, ko // 2, 128), F32),
            dma((6,)),
            dma((chunks, 2)),
            dma((chunks, fn)),
            dma((chunks, fn)),
            dma((chunks, fn)),
            dma((chunks, fn)),
            dma((chunks, fn)),
            dma((2,)),
            dma((2,)),
            dma((2,)),
            dma((n,)),
            dma((n,)),
        ],
        compiler_params=pltpu.CompilerParams(
            collective_id=0, has_side_effects=True, vmem_limit_bytes=48 * 1024 * 1024
        ),
    )(
        patches, cotangent, segment.reshape(1, rows), home_map, ln_gain.reshape(1, width),
        w_up, w_down_t, p_in1, q_out1, p_in2, q_out2,
    )


def solution(mesh):
    return jax.shard_map(
        body,
        mesh=mesh,
        in_specs=(
            P(("group", "fsdp", "seq"), None),
            P(("group", "fsdp", "seq"), None),
            P(("group", "fsdp", "seq")),
            P("group"),
            P(),
            P("fsdp", "proj"),
            P("fsdp", "proj"),
            P(),
            P("proj", None),
            P("proj", None),
            P(),
        ),
        out_specs=P(("group", "fsdp", "seq"), "proj", None),
        check_vma=False,
    )
```

time: 322 us -> 94.8 us (0.29)
  waiting for transfers between devices: 254 us -> 0 us
  Pallas kernels: 0 us -> 84.4 us
  blocking collectives: 30.6 us -> 0 us
  matrix products: 15.3 us -> 0 us
  between operations: 14 us -> 0.06 us
  local copies, waits for them, and re-layouts: 4.71 us -> 9.95 us
    all_gather x2 -> x0, waiting for transfers between devices: 233 us -> none  [the longest x1 122 us: body(): pre = add_rows(normed, lax.all_gather(w_up, 'fsdp', axis=0, tiled=True))]
    pallas_call x0 -> x1, Pallas kernels: none -> 84.4 us  [body(): pl.pallas_call(functools.partial(kernel, fn, sn, chunks), out_shape=jax.S...]
    unnamed x1 -> x0, blocking collectives: 30.6 us -> none
    reduce_scatter x1 -> x0, waiting for transfers between devices: 20.1 us -> none  [body(): lax.psum_scatter(split_rows, ('fsdp', 'seq', 'proj'), scatter_dimension=0...]
    dot_general x7 -> x0, matrix products: 15.3 us -> none  [the longest x1 7.23 us: body(): out_one = jnp.dot(dpre, q_out1, preferred_element_type=jnp.float32)]
    unnamed x24 -> x17, local copies, waits for them, and re-layouts: 3.83 us -> 8.43 us
  transfers between devices with their start and end apart: 3 -> 0, of which waited for: 3 -> 0; matrix products, arithmetic and copies ran while one was open for 3% -> 0% of each run, Pallas kernels for 0% -> 0%
where the time goes in v1:
time: 94.8 us; the launch traced here: 94.4 us
  Pallas kernels  84.4 us (89%)
  local copies, waits for them, and re-layouts  9.95 us (10%)
    pallas_call x1, Pallas kernels, body(): pl.pallas_call(functools.partial(kernel, fn, sn, chunks), out_shape=jax.S...  84.4 us
    unnamed x17, local copies, waits for them, and re-layouts  8.43 us

profile of v1, /device:TPU:0, one launch (start us, length us, event | category | flops | bytes accessed | tf_op | source)
XLA Modules:
  0.0 94.4 jit_solution(2805188522492973945)
XLA Ops:
  0.0 0.0 copy-start.5
  0.0 0.0 copy-start
  0.0 0.0 copy-start.4
  0.0 0.8 reshape.6.seg
  0.8 0.7 reshape.7.gain
  1.5 1.1 %copy.12.p_in1 = bf16[1280,32]{1,0:T(8,128)(2,1)S(1)} copy(bf16[1280,32]{0,1:T(8,128)(2,1)} %param.18) | data formatting | bytes 163840 | tf_op args[7]
  2.6 1.8 %copy.15.q_out2 = bf16[1280,32]{1,0:T(8,128)(2,1)} copy(bf16[1280,32]{0,1:T(8,128)(2,1)} %param.21) | data formatting | bytes 163840 | tf_op args[10]
  4.4 1.2 %copy.13.q_out1 = bf16[2560,32]{1,0:T(8,128)(2,1)S(1)} copy(bf16[2560,32]{0,1:T(8,128)(2,1)} %param.19) | data formatting | bytes 327680 | tf_op args[8]
  5.7 0.0 copy-done.5
  5.7 0.3 copy.14.p_in2
  6.0 0.0 copy-done
  6.0 0.0 copy-done.4
  6.0 0.0 copy-start.1
  6.0 1.0 %copy-done.1 = bf16[1280,32]{1,0:T(8,128)(2,1)S(1)} copy-done((bf16[1280,32]{1,0:T(8,128)(2,1)S(1)}, bf16[1280,32]{1,0:T(8,128)(2,1)}, u32[]{:S(2)}) %copy-start.1) | copy-done | bytes 81944
  7.0 0.0 copy-start.2
  7.0 1.2 %copy-done.2 = bf16[384,1280]{1,0:T(8,128)(2,1)S(1)} copy-done((bf16[384,1280]{1,0:T(8,128)(2,1)S(1)}, bf16[384,1280]{1,0:T(8,128)(2,1)}, u32[]{:S(2)}) %copy-start.2) | copy-done | bytes 983064
  8.2 0.0 copy-start.3
  8.2 1.2 %copy-done.3 = bf16[384,1280]{1,0:T(8,128)(2,1)S(1)} copy-done((bf16[384,1280]{1,0:T(8,128)(2,1)S(1)}, bf16[384,1280]{1,0:T(8,128)(2,1)}, u32[]{:S(2)}) %copy-start.3) | copy-done | bytes 983064
  9.4 84.4 %shard_map.109 = f32[1,16,64]{2,1,0:T(8,128)S(1)} custom-call(bf16[384,1280]{1,0:T(8,128)(2,1)S(1)} %copy-done.2, bf16[384,1280]{1,0:T(8,128)(2,1)S(1)} %copy-done.3, s32[1,384]{1,0:T(1,128)S(1)} %reshape.6.seg, s32[8]{0:T(128)S(1)} %copy-done.4, f32[1,1280]{1,0:T(1,128)S(1)} %reshape.7.gain, bf16[320,2560]{1,0:T(8,128)(2,1)S(1)} %copy-done, ...), custom_call_target="tpu_custom_call" | custom-call | tf_op jit(solution)/shard_map/pallas_call | solution.py:350
  93.8 0.6 copy.17
Async XLA Ops:
  0.0 5.7 %copy-start.5 = (bf16[2560,32]{0,1:T(8,128)(2,1)S(1)}, bf16[2560,32]{0,1:T(8,128)(2,1)}, u32[]{:S(2)}) copy-start(bf16[2560,32]{0,1:T(8,128)(2,1)} %param.20) | copy-start | bytes 491524
  0.0 6.0 %copy-start = (bf16[320,2560]{1,0:T(8,128)(2,1)S(1)}, bf16[320,2560]{1,0:T(8,128)(2,1)}, u32[]{:S(2)}) copy-start(bf16[320,2560]{1,0:T(8,128)(2,1)} %w_up.1) | copy-start | bytes 4915204
  0.0 6.0 %copy-start.4 = (s32[8]{0:T(128)S(1)}, s32[8]{0:T(128)}, u32[]{:S(2)}) copy-start(s32[8]{0:T(128)} %home.1) | copy-start | bytes 100
  6.0 1.0 %copy-start.1 = (bf16[1280,32]{1,0:T(8,128)(2,1)S(1)}, bf16[1280,32]{1,0:T(8,128)(2,1)}, u32[]{:S(2)}) copy-start(bf16[1280,32]{1,0:T(8,128)(2,1)} %copy.15.q_out2) | copy-start | bytes 245764
  7.0 1.2 %copy-start.2 = (bf16[384,1280]{1,0:T(8,128)(2,1)S(1)}, bf16[384,1280]{1,0:T(8,128)(2,1)}, u32[]{:S(2)}) copy-start(bf16[384,1280]{1,0:T(8,128)(2,1)} %patches.1) | copy-start | bytes 2949124
  8.2 1.2 %copy-start.3 = (bf16[384,1280]{1,0:T(8,128)(2,1)S(1)}, bf16[384,1280]{1,0:T(8,128)(2,1)}, u32[]{:S(2)}) copy-start(bf16[384,1280]{1,0:T(8,128)(2,1)} %cot.1) | copy-start | bytes 2949124

commit v2 on v1

v2 whole, which is shorter than its diff:
```python
import functools

import jax
import jax.numpy as jnp
from jax import lax
from jax.experimental import pallas as pl
from jax.experimental.pallas import tpu as pltpu
from jax.sharding import PartitionSpec as P

KC = 256
HC = 128
MESH = pl.DeviceIdType.MESH
BF = jnp.bfloat16
F32 = jnp.float32
NT = (((1,), (1,)), ((), ()))


def kernel(
    fn, sn, chunks, extra,
    patches, cot, seg, home, gain, w_up, w_down, p_in1, q_out1, p_in2, q_out2,
    out,
    pbuf, xbuf, sbuf, wbuf, p1p, p2p, q1t, q2t, in1, in2, t1, t2, part, gath,
    lsem, wsem, zrecv, yrecv, rsend, lsend, ysend, xsem, esem, csem, seg_sem, red_send, red_recv,
):
    g, f = lax.axis_index("group"), lax.axis_index("fsdp")
    s, p = lax.axis_index("seq"), lax.axis_index("proj")
    s2 = lax.rem(s, 2)
    mate = s + 1 - 2 * s2
    n = fn * sn * 2
    me = (f * sn + s) * 2 + p
    rows, width = patches.shape
    half = rows // 2
    depth = w_up.shape[0]
    images = home.shape[0]
    ko = q_out1.shape[0]
    ki = p_in1.shape[0]
    cols = chunks * KC
    base = pl.multiple_of(s2 * cols, KC)

    def spot(linear):
        return {"fsdp": linear // (2 * sn), "seq": lax.rem(linear // 2, sn), "proj": lax.rem(linear, 2)}

    own_rows = pl.ds(0, rows)
    loads = [
        pltpu.make_async_copy(patches, pbuf, lsem.at[0]),
        pltpu.make_async_copy(cot, xbuf.at[1, own_rows], lsem.at[1]),
        pltpu.make_async_copy(q_out1.at[:, pl.ds(base, cols)], q1t, lsem.at[2]),
        pltpu.make_async_copy(p_in2.at[:, pl.ds(base, cols)], p2p.at[pl.ds(ki, ki)], lsem.at[3]),
        pltpu.make_async_copy(p_in1, p1p.at[pl.ds(0, ki)], lsem.at[4]),
        pltpu.make_async_copy(q_out2, q2t, lsem.at[5]),
    ]

    p1p[ki:, :] = jnp.zeros((128 - ki, width), BF)
    p2p[:ki, :] = jnp.zeros((ki, cols), BF)
    p2p[2 * ki:, :] = jnp.zeros((128 - 2 * ki, cols), BF)

    def own_load(k, m, side):
        source = (w_up, w_down)[m]
        columns = pl.ds(pl.multiple_of(base + k * KC + side * HC, HC), HC)
        return pltpu.make_async_copy(
            source.at[:, columns], wbuf.at[k, side, m, pl.ds(pl.multiple_of(f * depth, depth), depth)],
            wsem.at[k, m, side],
        )

    for k in range(chunks):
        for m in range(2):
            for side in range(2):
                own_load(k, m, side).start()
        if k == 0:
            loads[1].start()
            loads[0].start()
    for load in loads[2:]:
        load.start()
    plain = chunks - extra
    middle = jnp.logical_and(f >= 1, f <= fn - 2)
    end = jnp.logical_not(middle)
    sbuf[0] = jnp.broadcast_to(seg[...].reshape(1, rows), sbuf.shape[1:])

    barrier = pltpu.get_barrier_semaphore()

    def greet(o, carry):
        pl.semaphore_signal(barrier, inc=1, device_id=spot(lax.rem(me + o, n)), device_id_type=MESH)
        return carry

    lax.fori_loop(1, n, greet, 0)
    pl.semaphore_signal(barrier, inc=1, device_id={"group": 1 - g}, device_id_type=MESH)
    pl.semaphore_wait(barrier, n)

    steps = plain + 2 * extra

    def piece(k, source, side):
        at = pl.ds(pl.multiple_of(source * depth, depth), depth)
        if k < plain:
            return wbuf.at[k, side, :, at]
        return wbuf.at[plain, k - plain, :, at]

    def z_copy(k, source, way):
        sems = rsend if way > 0 else lsend
        block = piece(k, source, g)
        return pltpu.make_async_remote_copy(
            src_ref=block, dst_ref=block, send_sem=sems.at[k, source], recv_sem=zrecv.at[k, source],
            device_id={"fsdp": f + way}, device_id_type=MESH,
        )

    def y_copy(k, source, side):
        block = piece(k, source, side)
        return pltpu.make_async_remote_copy(
            src_ref=block, dst_ref=block, send_sem=ysend.at[k, source], recv_sem=yrecv.at[k, source],
            device_id={"group": 1 - g}, device_id_type=MESH,
        )

    def to_right(k):
        return f < (fn - 1 if k < plain else fn - 2)

    def to_left(k):
        return f > (0 if k < plain else 1)

    def got(k, d):
        left, right = f - d >= 0, f + d < fn
        if k >= plain:
            left, right = jnp.logical_and(left, middle), jnp.logical_and(right, middle)
        return left, right

    def send_own(k):
        if k < plain or k == plain:
            for m in range(2):
                for side in range(2):
                    own_load(min(k, plain), m, side).wait()

        @pl.when(to_right(k))
        def _():
            z_copy(k, f, 1).start()

        @pl.when(to_left(k))
        def _():
            z_copy(k, f, -1).start()

    def forward(k):
        for d in range(1, fn):
            left, right = got(k, d)

            @pl.when(left)
            def _():
                z_copy(k, f - d, 1).wait_recv()

                @pl.when(to_right(k))
                def _():
                    z_copy(k, f - d, 1).start()

                if k < plain:
                    y_copy(k, f - d, g).start()

            @pl.when(right)
            def _():
                z_copy(k, f + d, -1).wait_recv()

                @pl.when(to_left(k))
                def _():
                    z_copy(k, f + d, -1).start()

                if k < plain:
                    y_copy(k, f + d, g).start()

    def half_of(m, block, side):
        return xbuf.at[m, pl.ds(pl.multiple_of(block * rows + side * half, half), half)]

    def x_copy(m, block):
        return pltpu.make_async_remote_copy(
            src_ref=half_of(m, block, p), dst_ref=half_of(m, block + 1, p),
            send_sem=xsem.at[0, m, block], recv_sem=xsem.at[1, m, block],
            device_id={"seq": mate}, device_id_type=MESH,
        )

    def c_copy(m, block, side):
        return pltpu.make_async_remote_copy(
            src_ref=half_of(m, block, side), dst_ref=half_of(m, block, side),
            send_sem=csem.at[0, m, block], recv_sem=csem.at[1, m, block],
            device_id={"proj": 1 - p}, device_id_type=MESH,
        )

    inward = jnp.where(f == 0, 1, fn - 2)

    def e_copy(m):
        return pltpu.make_async_remote_copy(
            src_ref=half_of(m, 0, p), dst_ref=half_of(m, 2, p), send_sem=esem.at[0, m], recv_sem=esem.at[1, m],
            device_id={"fsdp": inward}, device_id_type=MESH,
        )

    def seg_copy(source, target, where):
        return pltpu.make_async_remote_copy(
            src_ref=sbuf.at[source], dst_ref=sbuf.at[target], send_sem=seg_sem.at[0, target],
            recv_sem=seg_sem.at[1, target], device_id=where, device_id_type=MESH,
        )

    across = {"seq": mate}
    send_own(0)
    loads[1].wait()
    x_copy(1, 0).start()
    seg_copy(0, 1, across).start()
    if extra:
        @pl.when(end)
        def _():
            e_copy(1).start()
            seg_copy(0, 2, {"fsdp": inward}).start()

    send_own(1)
    loads[0].wait()
    step = 32
    scale = gain[...].reshape(1, width)

    def norm(i, carry):
        at = pl.ds(pl.multiple_of(i * step, step), step)
        values = pbuf[at, :].astype(F32)
        center = values - jnp.mean(values, axis=-1, keepdims=True)
        spread = jnp.mean(center * center, axis=-1, keepdims=True)
        xbuf[0, at, :] = (center * lax.rsqrt(spread + 1e-06) * scale).astype(BF)
        return carry

    lax.fori_loop(0, rows // step, norm, 0)
    x_copy(0, 0).start()
    if extra:
        @pl.when(end)
        def _():
            e_copy(0).start()

    for load in loads[2:]:
        load.wait()

    def small(r):
        at = pl.ds(r * rows, rows)
        in1[r] = lax.dot_general(xbuf[0, at, :], p1p[...], NT, preferred_element_type=F32)
        t2[r] = lax.dot_general(q2t[...], xbuf[1, at, :], NT, preferred_element_type=F32)

    def compute(k, low, high):
        for d in range(1, fn if k < plain else 1):
            @pl.when(f - d >= 0)
            def _():
                y_copy(k, f - d, 1 - g).wait_recv()

            @pl.when(f + d < fn)
            def _():
                y_copy(k, f + d, 1 - g).wait_recv()

        def rows_of(r, carry):
            at = pl.ds(pl.multiple_of(r * rows, rows), rows)
            up = jnp.concatenate([wbuf[k, 0, 0], wbuf[k, 1, 0]], axis=1)
            down = jnp.concatenate([wbuf[k, 0, 1], wbuf[k, 1, 1]], axis=1)
            pre = jnp.dot(xbuf[0, at, :], up, preferred_element_type=F32)
            dact = jnp.dot(xbuf[1, at, :], down, preferred_element_type=F32)
            sigma = 0.5 + 0.5 * jnp.tanh(0.851 * pre)
            act = (pre * sigma).astype(BF)
            dpre = (dact * (sigma * (1.0 + 1.702 * pre * (1.0 - sigma)))).astype(BF)
            two = lax.dot_general(act, p2p[:, k * KC:(k + 1) * KC], NT, preferred_element_type=F32)
            one = lax.dot_general(q1t[:, k * KC:(k + 1) * KC], dpre, NT, preferred_element_type=F32)
            if k == 0 or low == 2:
                in2[r] = two
                t1[r] = one
            else:
                in2[r] += two
                t1[r] += one
            return carry

        lax.fori_loop(low, high, rows_of, 0)

    def hand_on(m, block):
        c_copy(m, block, p).start()

    def from_end(m):
        if extra:
            @pl.when(middle)
            def _():
                e_copy(m).wait_recv()
                x_copy(m, 2).start()
                hand_on(m, 2)

    small(0)
    forward(0)
    send_own(2)
    forward(1)
    send_own(3)
    x_copy(1, 0).wait_recv()
    hand_on(1, 1)
    from_end(1)
    x_copy(0, 0).wait_recv()
    hand_on(0, 1)
    seg_copy(0, 1, across).wait_recv()
    c_copy(1, 1, 1 - p).wait_recv()
    c_copy(0, 1, 1 - p).wait_recv()
    if extra:
        @pl.when(middle)
        def _():
            seg_copy(0, 2, {"fsdp": inward}).wait_recv()
            seg_copy(2, 3, across).start()

    small(1)
    for k in range(2, steps):
        if k == 2:
            from_end(0)
        forward(k)
        if k + 2 < steps:
            send_own(k + 2)
        if k - 2 < plain - 1:
            compute(k - 2, 0, 2)
    for k in range(steps - 2, plain):
        compute(k, 0, 2)
    if extra:
        @pl.when(middle)
        def _():
            for m in (1, 0):
                x_copy(m, 2).wait_recv()
                hand_on(m, 3)

        compute(plain - 1, 0, 2)

        @pl.when(middle)
        def _():
            compute(plain, 0, 2)
            seg_copy(2, 3, across).wait_recv()
            for block in (2, 3):
                for m in (1, 0):
                    c_copy(m, block, 1 - p).wait_recv()
                small(block)
            compute(plain, 2, 4)

    lane = lax.broadcasted_iota(jnp.int32, (ko // 2, 128), 1)
    many = 8

    def blocks(b, carry):
        def add(r, sums):
            raw, counts = sums
            ids = sbuf[r, 0:1, :]
            goal = lax.fori_loop(
                0, images, lambda e, t: jnp.where(ids == e, home[e], t), jnp.zeros_like(ids), unroll=images <= 8
            )
            marks = [(goal == b * many + j).astype(F32) for j in range(many)]
            own = (r < 2).astype(F32)
            counts = tuple(c + own * jnp.sum(m, axis=1, keepdims=True) for c, m in zip(counts, marks))
            left1 = jnp.concatenate([t1[r] * m for m in marks], axis=0)
            left2 = jnp.concatenate([t2[r] * m for m in marks], axis=0)
            raw += jnp.dot(left1, in1[r], preferred_element_type=F32, precision=lax.Precision.HIGHEST)
            raw += jnp.dot(left2, in2[r], preferred_element_type=F32, precision=lax.Precision.HIGHEST)
            return raw, counts

        blank = (jnp.zeros((many * ko, 128), F32), (jnp.zeros((1, 1), F32),) * many)
        raw, counts = lax.fori_loop(0, jnp.where(middle, 4, 2) if extra else 2, add, blank)
        for j in range(many):
            for c in range(2):
                start = j * ko + c * (ko // 2)
                part[(b * many + j) * 2 + c] = jnp.where(
                    lane == 2 * ki, counts[j], raw[start:start + ko // 2]
                )
        return carry

    lax.fori_loop(0, images // many, blocks, 0)

    def give(o):
        target = lax.rem(me + o, n)
        return pltpu.make_async_remote_copy(
            src_ref=part.at[target], dst_ref=gath.at[me], send_sem=red_send.at[target], recv_sem=red_recv.at[me],
            device_id=spot(target), device_id_type=MESH,
        )

    def take(o):
        origin = lax.rem(me + n - o, n)
        return origin, pltpu.make_async_remote_copy(
            src_ref=part.at[origin], dst_ref=gath.at[origin], send_sem=red_send.at[origin],
            recv_sem=red_recv.at[origin], device_id=spot(origin), device_id_type=MESH,
        )

    def start(o, carry):
        give(o).start()
        return carry

    lax.fori_loop(1, n, start, 0)

    def finish(o, total):
        origin, copy = take(o)
        copy.wait_recv()
        return total + gath[origin]

    total = lax.fori_loop(1, n, finish, part[me])
    out[0] = total[:, :2 * ki] * lax.rsqrt(total[:, 2 * ki:2 * ki + 1] * 0.25)

    def drain(o, carry):
        give(o).wait_send()
        return carry

    lax.fori_loop(1, n, drain, 0)
    for m in range(2):
        x_copy(m, 0).wait_send()
        c_copy(m, 1, p).wait_send()
    seg_copy(0, 1, across).wait_send()
    if extra:
        @pl.when(end)
        def _():
            for m in range(2):
                e_copy(m).wait_send()
            seg_copy(0, 2, {"fsdp": inward}).wait_send()

        @pl.when(middle)
        def _():
            for m in range(2):
                x_copy(m, 2).wait_send()
                c_copy(m, 2, p).wait_send()
                c_copy(m, 3, p).wait_send()
            seg_copy(2, 3, across).wait_send()

    for k in range(steps):
        @pl.when(to_right(k))
        def _():
            z_copy(k, f, 1).wait_send()

        @pl.when(to_left(k))
        def _():
            z_copy(k, f, -1).wait_send()

        for d in range(1, fn):
            left, right = got(k, d)

            @pl.when(left)
            def _():
                @pl.when(to_right(k))
                def _():
                    z_copy(k, f - d, 1).wait_send()

                if k < plain:
                    y_copy(k, f - d, g).wait_send()

            @pl.when(right)
            def _():
                @pl.when(to_left(k))
                def _():
                    z_copy(k, f + d, -1).wait_send()

                if k < plain:
                    y_copy(k, f + d, g).wait_send()


def body(
    patches, cotangent, segment, home_map, ln_gain, w_up, w_down_t, p_in1, q_out1, p_in2, q_out2
):
    fn, sn = lax.axis_size("fsdp"), lax.axis_size("seq")
    n = fn * sn * 2
    rows, width = patches.shape
    cols = w_up.shape[1] // 2
    chunks = cols // KC
    extra = 1 if fn == 4 else 0
    blocks = 2 + 2 * extra
    steps = chunks + extra
    ko, ki = q_out1.shape[1], p_in1.shape[1]
    any_ = pl.BlockSpec(memory_space=pltpu.HBM)
    vmem = pl.BlockSpec(memory_space=pltpu.VMEM)
    smem = pl.BlockSpec(memory_space=pltpu.SMEM)
    dma = pltpu.SemaphoreType.DMA
    return pl.pallas_call(
        functools.partial(kernel, fn, sn, chunks, extra),
        out_shape=jax.ShapeDtypeStruct((1, ko // 2, 2 * ki), F32),
        in_specs=[any_, any_, vmem, smem, vmem, any_, any_, any_, any_, any_, any_],
        out_specs=vmem,
        scratch_shapes=[
            pltpu.VMEM((rows, width), BF),
            pltpu.VMEM((2, blocks * rows, width), BF),
            pltpu.VMEM((blocks, 8, rows), jnp.int32),
            pltpu.VMEM((chunks, 2, 2, width, HC), BF),
            pltpu.VMEM((128, width), BF),
            pltpu.VMEM((128, cols), BF),
            pltpu.VMEM((ko, cols), BF),
            pltpu.VMEM((ko, width), BF),
            pltpu.VMEM((blocks, rows, 128), F32),
            pltpu.VMEM((blocks, rows, 128), F32),
            pltpu.VMEM((blocks, ko, rows), F32),
            pltpu.VMEM((blocks, ko, rows), F32),
            pltpu.VMEM((n, ko // 2, 128), F32),
            pltpu.VMEM((n, ko // 2, 128), F32),
            dma((6,)),
            dma((chunks, 2, 2)),
            dma((steps, fn)),
            dma((steps, fn)),
            dma((steps, fn)),
            dma((steps, fn)),
            dma((steps, fn)),
            dma((2, 2, blocks)),
            dma((2, 2)),
            dma((2, 2, blocks)),
            dma((2, blocks)),
            dma((n,)),
            dma((n,)),
        ],
        compiler_params=pltpu.CompilerParams(
            collective_id=0, has_side_effects=True, vmem_limit_bytes=63 * 1024 * 1024
        ),
    )(
        patches, cotangent, segment, home_map, ln_gain,
        w_up, w_down_t, p_in1.T, q_out1.T, p_in2.T, q_out2.T,
    )


def solution(mesh):
    return jax.shard_map(
        body,
        mesh=mesh,
        in_specs=(
            P(("group", "fsdp", "seq"), None),
            P(("group", "fsdp", "seq"), None),
            P(("group", "fsdp", "seq")),
            P("group"),
            P(),
            P("fsdp", "proj"),
            P("fsdp", "proj"),
            P(),
            P("proj", None),
            P("proj", None),
            P(),
        ),
        out_specs=P(("group", "fsdp", "seq"), "proj", None),
        check_vma=False,
    )
```

time: 94.8 us -> 84.5 us (0.89)
  local copies, waits for them, and re-layouts: 9.95 us -> 1.3 us
  Pallas kernels: 84.4 us -> 83 us
    unnamed x17 -> x1, local copies, waits for them, and re-layouts: 8.43 us -> 1.3 us
    reshape x2 -> x0, local copies, waits for them, and re-layouts: 1.52 us -> none  [the longest x1 0.81 us: body(): segment.reshape(1, rows)]
    pallas_call x1, Pallas kernels: 84.4 us -> 83 us  [body(): pl.pallas_call(functools.partial(kernel, fn, sn, chunks, extra), out_shap...]
where the time goes in v2:
time: 84.5 us; the launch traced here: 84.3 us
  Pallas kernels  83 us (98%)
  local copies, waits for them, and re-layouts  1.3 us (2%)
    pallas_call x1, Pallas kernels, body(): pl.pallas_call(functools.partial(kernel, fn, sn, chunks, extra), out_shap...  83 us

profile of v2, /device:TPU:0, one launch (start us, length us, event | category | flops | bytes accessed | tf_op | source)
XLA Modules:
  0.0 84.3 jit_solution(15110879395775623186)
XLA Ops:
  0.0 83.0 %shard_map.109 = f32[1,16,64]{2,1,0:T(8,128)} custom-call(bf16[384,1280]{1,0:T(8,128)(2,1)} %patches.1, bf16[384,1280]{1,0:T(8,128)(2,1)} %cot.1, s32[384]{0:T(512)} %seg.1, s32[8]{0:T(128)} %home.1, f32[1280]{0:T(1024)} %gain.1, bf16[320,2560]{1,0:T(8,128)(2,1)} %w_up.1, bf16[320,2560]{1,0:T(8,128)(2,1)} %w_down.1, bf16[32,1280]{1,0:T(8,128)(2,1)} %bitcast.6, ...), custom_call_target="tpu_custom_call" | custom-call | tf_op jit(solution)/shard_map/pallas_call | solution.py:455
  83.0 1.3 %copy.13 = f32[1,16,64]{2,1,0:T(8,128)} copy(f32[1,16,64]{2,1,0:T(8,128)} %shard_map.109) | data formatting | bytes 8192

commit v3 on v2

--- a/solution.py
+++ b/solution.py
@@ -40,6 +40,15 @@
     def spot(linear):
         return {"fsdp": linear // (2 * sn), "seq": lax.rem(linear // 2, sn), "proj": lax.rem(linear, 2)}
 
+    barrier = pltpu.get_barrier_semaphore()
+
+    def greet(o, carry):
+        pl.semaphore_signal(barrier, inc=1, device_id=spot(lax.rem(me + o, n)), device_id_type=MESH)
+        return carry
+
+    lax.fori_loop(1, n, greet, 0)
+    pl.semaphore_signal(barrier, inc=1, device_id={"group": 1 - g}, device_id_type=MESH)
+
     own_rows = pl.ds(0, rows)
     loads = [
         pltpu.make_async_copy(patches, pbuf, lsem.at[0]),
@@ -76,14 +85,6 @@
     end = jnp.logical_not(middle)
     sbuf[0] = jnp.broadcast_to(seg[...].reshape(1, rows), sbuf.shape[1:])
 
-    barrier = pltpu.get_barrier_semaphore()
-
-    def greet(o, carry):
-        pl.semaphore_signal(barrier, inc=1, device_id=spot(lax.rem(me + o, n)), device_id_type=MESH)
-        return carry
-
-    lax.fori_loop(1, n, greet, 0)
-    pl.semaphore_signal(barrier, inc=1, device_id={"group": 1 - g}, device_id_type=MESH)
     pl.semaphore_wait(barrier, n)
 
     steps = plain + 2 * extra
@@ -252,7 +253,7 @@
             dpre = (dact * (sigma * (1.0 + 1.702 * pre * (1.0 - sigma)))).astype(BF)
             two = lax.dot_general(act, p2p[:, k * KC:(k + 1) * KC], NT, preferred_element_type=F32)
             one = lax.dot_general(q1t[:, k * KC:(k + 1) * KC], dpre, NT, preferred_element_type=F32)
-            if k == 0 or low == 2:
+            if k == 0 or low >= 2:
                 in2[r] = two
                 t1[r] = one
             else:
@@ -304,23 +305,23 @@
     for k in range(steps - 2, plain):
         compute(k, 0, 2)
     if extra:
+        compute(plain - 1, 0, 2)
+
         @pl.when(middle)
         def _():
+            for m in (1, 0):
+                c_copy(m, 2, 1 - p).wait_recv()
+            small(2)
             for m in (1, 0):
                 x_copy(m, 2).wait_recv()
                 hand_on(m, 3)
-
-        compute(plain - 1, 0, 2)
-
-        @pl.when(middle)
-        def _():
             compute(plain, 0, 2)
+            compute(plain, 2, 3)
             seg_copy(2, 3, across).wait_recv()
-            for block in (2, 3):
-                for m in (1, 0):
-                    c_copy(m, block, 1 - p).wait_recv()
-                small(block)
-            compute(plain, 2, 4)
+            for m in (1, 0):
+                c_copy(m, 3, 1 - p).wait_recv()
+            small(3)
+            compute(plain, 3, 4)
 
     lane = lax.broadcasted_iota(jnp.int32, (ko // 2, 128), 1)
     many = 8
@@ -373,19 +374,6 @@
 
     lax.fori_loop(1, n, start, 0)
 
-    def finish(o, total):
-        origin, copy = take(o)
-        copy.wait_recv()
-        return total + gath[origin]
-
-    total = lax.fori_loop(1, n, finish, part[me])
-    out[0] = total[:, :2 * ki] * lax.rsqrt(total[:, 2 * ki:2 * ki + 1] * 0.25)
-
-    def drain(o, carry):
-        give(o).wait_send()
-        return carry
-
-    lax.fori_loop(1, n, drain, 0)
     for m in range(2):
         x_copy(m, 0).wait_send()
         c_copy(m, 1, p).wait_send()
@@ -434,6 +422,20 @@
 
                 if k < plain:
                     y_copy(k, f + d, g).wait_send()
+
+    def finish(o, total):
+        origin, copy = take(o)
+        copy.wait_recv()
+        return total + gath[origin]
+
+    total = lax.fori_loop(1, n, finish, part[me])
+    out[0] = total[:, :2 * ki] * lax.rsqrt(total[:, 2 * ki:2 * ki + 1] * 0.25)
+
+    def drain(o, carry):
+        give(o).wait_send()
+        return carry
+
+    lax.fori_loop(1, n, drain, 0)
 
 
 def body(

time: 84.5 us -> 84.2 us (level)
  no operation moved by 1% of the time
where the time goes in v3:
time: 84.2 us; the launch traced here: 84 us
  Pallas kernels  82.7 us (98%)
  local copies, waits for them, and re-layouts  1.3 us (2%)
    pallas_call x1, Pallas kernels, body(): pl.pallas_call(functools.partial(kernel, fn, sn, chunks, extra), out_shap...  82.7 us

profile of v3, /device:TPU:0, one launch (start us, length us, event | category | flops | bytes accessed | tf_op | source)
XLA Modules:
  0.0 84.0 jit_solution(8494825118982528577)
XLA Ops:
  0.0 82.7 %shard_map.109 = f32[1,16,64]{2,1,0:T(8,128)} custom-call(bf16[384,1280]{1,0:T(8,128)(2,1)} %patches.1, bf16[384,1280]{1,0:T(8,128)(2,1)} %cot.1, s32[384]{0:T(512)} %seg.1, s32[8]{0:T(128)} %home.1, f32[1280]{0:T(1024)} %gain.1, bf16[320,2560]{1,0:T(8,128)(2,1)} %w_up.1, bf16[320,2560]{1,0:T(8,128)(2,1)} %w_down.1, bf16[32,1280]{1,0:T(8,128)(2,1)} %bitcast.6, ...), custom_call_target="tpu_custom_call" | custom-call | tf_op jit(solution)/shard_map/pallas_call | solution.py:457
  82.7 1.3 %copy.13 = f32[1,16,64]{2,1,0:T(8,128)} copy(f32[1,16,64]{2,1,0:T(8,128)} %shard_map.109) | data formatting | bytes 8192

commit v4 on v3

--- a/solution.py
+++ b/solution.py
@@ -194,7 +194,6 @@
         )
 
     across = {"seq": mate}
-    send_own(0)
     loads[1].wait()
     x_copy(1, 0).start()
     seg_copy(0, 1, across).start()
@@ -204,7 +203,7 @@
             e_copy(1).start()
             seg_copy(0, 2, {"fsdp": inward}).start()
 
-    send_own(1)
+    send_own(0)
     loads[0].wait()
     step = 32
     scale = gain[...].reshape(1, width)
@@ -224,6 +223,7 @@
         def _():
             e_copy(0).start()
 
+    send_own(1)
     for load in loads[2:]:
         load.wait()
 

time: 84.2 us -> 91.5 us (1.087)
  Pallas kernels: 82.7 us -> 90 us
    pallas_call x1, Pallas kernels: 82.7 us -> 90 us  [body(): pl.pallas_call(functools.partial(kernel, fn, sn, chunks, extra), out_shap...]
where the time goes in v4:
time: 91.5 us; the launch traced here: 91.3 us
  Pallas kernels  90 us (98%)
  local copies, waits for them, and re-layouts  1.3 us (1%)
    pallas_call x1, Pallas kernels, body(): pl.pallas_call(functools.partial(kernel, fn, sn, chunks, extra), out_shap...  90 us

profile of v4, /device:TPU:0, one launch (start us, length us, event | category | flops | bytes accessed | tf_op | source)
XLA Modules:
  0.0 91.3 jit_solution(13978308107587824845)
XLA Ops:
  0.0 90.0 %shard_map.109 = f32[1,16,64]{2,1,0:T(8,128)} custom-call(bf16[384,1280]{1,0:T(8,128)(2,1)} %patches.1, bf16[384,1280]{1,0:T(8,128)(2,1)} %cot.1, s32[384]{0:T(512)} %seg.1, s32[8]{0:T(128)} %home.1, f32[1280]{0:T(1024)} %gain.1, bf16[320,2560]{1,0:T(8,128)(2,1)} %w_up.1, bf16[320,2560]{1,0:T(8,128)(2,1)} %w_down.1, bf16[32,1280]{1,0:T(8,128)(2,1)} %bitcast.6, ...), custom_call_target="tpu_custom_call" | custom-call | tf_op jit(solution)/shard_map/pallas_call | solution.py:457
  90.0 1.3 %copy.13 = f32[1,16,64]{2,1,0:T(8,128)} copy(f32[1,16,64]{2,1,0:T(8,128)} %shard_map.109) | data formatting | bytes 8192
